TPU v7x, 32 devices: a whole 2x2x4 slice. The times are simulated.
32 devices in a mesh: energy: 8 (over z, y), momentum: 4 (over x, core).
Axes of the slice: x: 2, y: 2, z: 4, core: 2. Of those that a mesh axis runs over, the one named last changes fastest.
Arguments:
- lesser: bfloat16 [8, 4, 2, 512, 512], P('energy', 'momentum'), may hold values from -6 to 6
- greater: bfloat16 [8, 4, 2, 512, 512], P('energy', 'momentum'), may hold values from -6 to 6
- retarded: bfloat16 [8, 4, 2, 512, 512], P('energy', 'momentum'), may hold values from -4.1875 to 4.1875
- occupation: float32 [2], replicated, may hold values from 0.1 to 2
- shift_slots: int32 [2, 2, 8], replicated, may hold values from 0 to 8, as said below
- coupling: int32 [2, 4, 4], replicated, may hold values from 1 to 8
Outputs:
- lesser_new: bfloat16 [8, 4, 2, 512, 512], P('energy', 'momentum')
- greater_new: bfloat16 [8, 4, 2, 512, 512], P('energy', 'momentum')
- retarded_new: bfloat16 [8, 4, 2, 512, 512], P('energy', 'momentum')
Inputs may be any that keep to these rules, and one draw needn't show every extreme that they name: The energies of the grid are held in slots in an order of their own, one energy a slot. Mode m has one shift, the same for all slots: shift_slots[m, 0, j] is the slot of the energy that lies that shift below the energy of slot j, shift_slots[m, 1, j] the slot of the energy as far above it, and 8 where that energy lies outside the grid.
All inputs are finite; a program needn't handle non-finite values.
Results may differ from a plain program's by a relative error of at most 0.0064.
Values may be sent and summed in bfloat16 or wider, within the bound.
A program may use at most 64 MiB of HBM per device.

v0:
```python
import jax
import jax.numpy as jnp
from jax import lax
from jax.sharding import PartitionSpec as P


def matrix_product(former, latter):
    return jnp.matmul(former, latter, preferred_element_type=jnp.float32)


def complex_product(former, latter):
    former_re = former[..., 0, :, :]
    former_im = former[..., 1, :, :]
    latter_re = latter[..., 0, :, :]
    latter_im = latter[..., 1, :, :]
    real_part = matrix_product(former_re, latter_re) - matrix_product(former_im, latter_im)
    imag_part = matrix_product(former_re, latter_im) + matrix_product(former_im, latter_re)
    return jnp.stack([real_part, imag_part], axis=-3)


def adjoint_product(former, propagator):
    former_re = former[..., 0, :, :]
    former_im = former[..., 1, :, :]
    prop_re = jnp.swapaxes(propagator[..., 0, :, :], -1, -2)
    prop_im = jnp.swapaxes(propagator[..., 1, :, :], -1, -2)
    real_part = matrix_product(former_re, prop_re) + matrix_product(former_im, prop_im)
    imag_part = matrix_product(former_im, prop_re) - matrix_product(former_re, prop_im)
    return jnp.stack([real_part, imag_part], axis=-3)


def scattering(less_part, more_part, weights, occupation, shift_slots):
    slots = less_part.shape[0]
    slot_ids = jnp.arange(slots, dtype=jnp.int32)
    picked = (shift_slots[..., None] == slot_ids).astype(jnp.float32)
    phonons = occupation[:, None, None]
    pick_less = phonons * picked[:, 0] + (phonons + 1.0) * picked[:, 1]
    pick_more = (phonons + 1.0) * picked[:, 0] + phonons * picked[:, 1]
    mixer_less = jnp.einsum("mjs,mkq->jksq", pick_less, weights, precision=lax.Precision.HIGHEST)
    mixer_more = jnp.einsum("mjs,mkq->jksq", pick_more, weights, precision=lax.Precision.HIGHEST)
    total_less = jnp.einsum(
        "jksq,sqxab->jkxab",
        mixer_less,
        less_part.astype(jnp.float32),
        precision=lax.Precision.HIGHEST,
    )
    total_more = jnp.einsum(
        "jksq,sqxab->jkxab",
        mixer_more,
        more_part.astype(jnp.float32),
        precision=lax.Precision.HIGHEST,
    )
    return (total_less, total_more)


def per_device(lesser, greater, retarded, occupation, shift_slots, coupling):
    momenta = coupling.shape[1]
    modes = coupling.shape[0]
    order = lesser.shape[3]
    factor = 1.0 / (order * 4.0 * (modes * momenta) ** 0.5)
    weights = coupling.astype(jnp.float32)
    rows_less, rows_more = (
        lax.all_to_all(lesser, "energy", split_axis=3, concat_axis=0, tiled=True),
        lax.all_to_all(greater, "energy", split_axis=3, concat_axis=0, tiled=True),
    )
    own_index = lax.axis_index("momentum")
    pieces = (
        lax.all_gather(rows_less, "momentum", axis=1, tiled=True),
        lax.all_gather(rows_more, "momentum", axis=1, tiled=True),
    )
    count = pieces[0].shape[1]
    chosen = lax.dynamic_slice(weights, (0, own_index, 0), (modes, 1, count))
    add_less, add_more = scattering(pieces[0], pieces[1], chosen, occupation, shift_slots)
    sigma_less = (add_less * factor).astype(jnp.bfloat16)
    sigma_more = (add_more * factor).astype(jnp.bfloat16)
    sigma_less, sigma_more = (
        lax.all_to_all(sigma_less, "energy", split_axis=0, concat_axis=3, tiled=True),
        lax.all_to_all(sigma_more, "energy", split_axis=0, concat_axis=3, tiled=True),
    )
    sigma_ret = ((sigma_more.astype(jnp.float32) - sigma_less.astype(jnp.float32)) * 0.5).astype(
        jnp.bfloat16
    )
    stacked = jnp.stack([sigma_less, sigma_more, sigma_ret])
    halfway = complex_product(retarded[None], stacked).astype(jnp.bfloat16)
    lesser_new = adjoint_product(halfway[0], retarded).astype(jnp.bfloat16)
    greater_new = adjoint_product(halfway[1], retarded).astype(jnp.bfloat16)
    retarded_new = (retarded.astype(jnp.float32) + complex_product(halfway[2], retarded)).astype(
        jnp.bfloat16
    )
    return (lesser_new, greater_new, retarded_new)


def solution(mesh):
    return jax.shard_map(
        per_device,
        mesh=mesh,
        in_specs=(
            P("energy", "momentum", None, None, None),
            P("energy", "momentum", None, None, None),
            P("energy", "momentum", None, None, None),
            P(),
            P(),
            P(),
        ),
        out_specs=(
            P("energy", "momentum", None, None, None),
            P("energy", "momentum", None, None, None),
            P("energy", "momentum", None, None, None),
        ),
        check_vma=False,
    )
```

profile of v0, /device:TPU:0, one launch (start us, length us, event | category | flops | bytes accessed | tf_op | source)
XLA Modules:
  0.0 179.2 jit_solution(12115761878033358903)
XLA Ops:
  7.2 0.0 all-gather.5.cloned.1.call-start
  7.2 2.3 %copy.29 = bf16[1,1,2,512,512]{4,2,1,0,3:T(2,128)(2,1)S(1)} copy(bf16[1,1,2,512,512]{4,3,2,1,0:T(8,128)(2,1)} %param.6) | data formatting | bytes 2097152 | tf_op args[0]
  9.5 0.0 copy-start.1
  9.5 33.0 %all_to_all.66 = bf16[1,1,2,512,512]{4,2,1,0,3:T(2,128)(2,1)S(1)} all-to-all(bf16[1,1,2,512,512]{4,2,1,0,3:T(2,128)(2,1)S(1)} %copy.29), channel_id=1, replica_groups=mesh['energy'=8,'momentum'=4] {'energy'}, dimensions={3} | all-to-all | bytes 2097152 | tf_op jit(solution)/shard_map/all_to_all | solution.py:62
  42.5 1.5 copy.69
  44.1 0.0 all-gather.5.cloned.1.call-update
  44.1 0.0 all-gather.7.cloned.1.call-start
  44.1 0.0 copy-done.1
  44.1 1.1 copy.36
  45.2 0.0 copy-start.2
  45.2 0.0 copy-start.3
  45.3 28.8 %all_to_all.67 = bf16[1,1,2,512,512]{4,2,1,0,3:T(2,128)(2,1)S(1)} all-to-all(bf16[1,1,2,512,512]{4,2,1,0,3:T(2,128)(2,1)S(1)} %copy.36), channel_id=1, replica_groups=mesh['energy'=8,'momentum'=4] {'energy'}, dimensions={3} | all-to-all | bytes 2097152 | tf_op jit(solution)/shard_map/all_to_all | solution.py:63
  74.1 1.5 copy.68
  75.7 0.0 all-gather.7.cloned.1.call-update
  75.7 0.0 copy-done.2
  75.7 0.7 dynamic-slice_convert_fusion
  76.4 0.0 copy-done.3
  76.4 0.1 fusion.68
  76.5 0.1 add_bitcast_fusion
  76.6 0.2 convolution_bitcast_fusion.1
  76.8 1.0 all-gather.5.cloned.1.call-done
  77.8 9.7 %fusion.15 = bf16[8,1,2,64,512]{4,0,3,2,1:T(8,128)(2,1)S(1)} fusion(bf16[8,4,1,2,64,512]{5,0,1,4,3,2:T(8,128)(2,1)} %all-gather.5.cloned.1.call-done, f32[8,8,4,1,1]{1,2,0,4,3:T(4,128)S(1)} %convolution_bitcast_fusion.1), kind=kOutput, calls=%fused_computation.24 | convolution fusion | flops 202375168 | bytes 5243904 | tf_op jit(solution)/shard_map/jksq,sqxab->jkxab/dot_general | solution.py:40
  87.4 1.3 copy.33
  88.7 5.5 %all-to-all-start.1 = ((bf16[8,1,2,64,512]{4,3,2,1,0:T(8,128)(2,1)}), bf16[8,1,2,64,512]{4,3,2,1,0:T(8,128)(2,1)S(1)}, u32[]{:S(2)}, u32[]{:S(2)}) async-start(bf16[8,1,2,64,512]{4,3,2,1,0:T(8,128)(2,1)} %copy.33), calls=%async_computation.1 | async-start | bytes 2097152 | tf_op jit(solution)/shard_map/all_to_all | solution.py:76
  94.2 0.2 convolution_bitcast_fusion
  94.4 20.0 %all-gather.7.cloned.1.call-done = bf16[8,4,1,2,64,512]{5,0,1,4,3,2:T(8,128)(2,1)} async-done(((bf16[8,1,1,2,64,512]{5,0,1,4,3,2:T(8,128)(2,1)}), bf16[8,4,1,2,64,512]{5,0,1,4,3,2:T(8,128)(2,1)}) %all-gather.7.cloned.1.call-update) | async-done | bytes 4194320 | tf_op jit(solution)/shard_map/all_gather | solution.py:68
  114.4 9.7 %fusion.18 = bf16[8,1,2,64,512]{4,0,3,2,1:T(8,128)(2,1)S(1)} fusion(bf16[8,4,1,2,64,512]{5,0,1,4,3,2:T(8,128)(2,1)} %all-gather.7.cloned.1.call-done, f32[8,8,4,1,1]{1,2,0,4,3:T(4,128)S(1)} %convolution_bitcast_fusion), kind=kOutput, calls=%fused_computation.25 | convolution fusion | flops 202375168 | bytes 5243904 | tf_op jit(solution)/shard_map/jksq,sqxab->jkxab/dot_general | solution.py:46
  124.0 1.3 copy.40
  125.3 0.0 all-to-all-done.1
  125.3 5.5 %all-to-all-start.3 = ((bf16[8,1,2,64,512]{4,3,2,1,0:T(8,128)(2,1)}), bf16[8,1,2,64,512]{4,3,2,1,0:T(8,128)(2,1)S(1)}, u32[]{:S(2)}, u32[]{:S(2)}) async-start(bf16[8,1,2,64,512]{4,3,2,1,0:T(8,128)(2,1)} %copy.40), calls=%async_computation.3 | async-start | bytes 2097152 | tf_op jit(solution)/shard_map/all_to_all | solution.py:77
  130.8 0.1 copy.34
  130.9 0.5 copy.44
  131.5 25.5 %all-to-all-done.3 = bf16[8,1,2,64,512]{4,3,2,1,0:T(8,128)(2,1)S(1)} async-done(((bf16[8,1,2,64,512]{4,3,2,1,0:T(8,128)(2,1)}), bf16[8,1,2,64,512]{4,3,2,1,0:T(8,128)(2,1)S(1)}, u32[]{:S(2)}, u32[]{:S(2)}) %all-to-all-start.3) | async-done | bytes 1048608 | tf_op jit(solution)/shard_map/all_to_all | solution.py:77
  157.0 0.1 copy.41
  157.1 0.5 copy.45
  157.7 0.3 multiply_convert_fusion
  158.0 0.0 copy-start
  158.0 0.3 pad_maximum_fusion
  158.4 0.9 copy-done
  159.2 1.0 fusion.14
  160.2 1.0 fusion.13
  161.3 1.1 fusion.12
  162.3 1.1 fusion.11
  163.4 0.3 fusion.35
  163.7 0.5 fusion.36
  164.1 0.5 fusion.40
  164.6 0.5 fusion.50
  165.1 0.5 fusion.52
  165.6 0.5 fusion.46
  166.1 0.5 fusion.48
  166.6 0.5 fusion.21
  167.0 0.5 fusion.22
  167.5 0.5 fusion.29
  168.0 0.5 fusion.30
  168.5 0.5 fusion.27
  169.0 0.5 fusion.28
  169.5 1.4 fusion.4
  170.8 1.5 pad_maximum_fusion.2
  (2 shorter events, 0.0 us)
Async XLA Ops:
  7.2 70.6 %all-gather.5.cloned.1.call-start = ((), (), s32[]{:S(2)}) async-start(), calls=%async_computation.4 | async-start | bytes 5242880 | tf_op jit(solution)/shard_map/all_gather | solution.py:67
  9.5 34.6 %copy-start.1 = (bf16[1,1,2,512,512]{4,3,2,1,0:T(8,128)(2,1)S(1)}, bf16[1,1,2,512,512]{4,3,2,1,0:T(8,128)(2,1)}, u32[]{:S(2)}) copy-start(bf16[1,1,2,512,512]{4,3,2,1,0:T(8,128)(2,1)} %param.7) | copy-start | bytes 3145732
  44.1 70.3 %all-gather.7.cloned.1.call-start = ((), (), s32[]{:S(2)}) async-start(), calls=%async_computation.5 | async-start | bytes 5242880 | tf_op jit(solution)/shard_map/all_gather | solution.py:68
  45.2 30.5 %copy-start.2 = (s32[2,2,8]{2,1,0:T(2,128)S(1)}, s32[2,2,8]{2,1,0:T(2,128)}, u32[]{:S(2)}) copy-start(s32[2,2,8]{2,1,0:T(2,128)} %param.10) | copy-start | bytes 388
  45.2 31.2 %copy-start.3 = (f32[2]{0:T(128)S(1)}, f32[2]{0:T(128)}, u32[]{:S(2)}) copy-start(f32[2]{0:T(128)} %param.9) | copy-start | bytes 28
  88.7 36.6 %all-to-all-start.1 = ((bf16[8,1,2,64,512]{4,3,2,1,0:T(8,128)(2,1)}), bf16[8,1,2,64,512]{4,3,2,1,0:T(8,128)(2,1)S(1)}, u32[]{:S(2)}, u32[]{:S(2)}) async-start(bf16[8,1,2,64,512]{4,3,2,1,0:T(8,128)(2,1)} %copy.33), calls=%async_computation.1 | async-start | bytes 2097152 | tf_op jit(solution)/shard_map/all_to_all | solution.py:76
  125.3 31.7 %all-to-all-start.3 = ((bf16[8,1,2,64,512]{4,3,2,1,0:T(8,128)(2,1)}), bf16[8,1,2,64,512]{4,3,2,1,0:T(8,128)(2,1)S(1)}, u32[]{:S(2)}, u32[]{:S(2)}) async-start(bf16[8,1,2,64,512]{4,3,2,1,0:T(8,128)(2,1)} %copy.40), calls=%async_computation.3 | async-start | bytes 2097152 | tf_op jit(solution)/shard_map/all_to_all | solution.py:77
  158.0 1.2 copy-start
Sparse Core Ops, SparseCore 0:
  44.2 33.5 all-gather.4
  79.9 34.4 all-gather.6
where the time goes:
time: 180 us; the launch traced here: 179 us
  blocking collectives  61.8 us (34%)
  waiting for transfers between devices  46.5 us (26%)
  matrix products  29.6 us (16%)
  between operations  14.3 us (8%)
  local copies, waits for them, and re-layouts  11.2 us (6%)
  starting transfers between devices  11.1 us (6%)
  other arithmetic  4.65 us (3%)
    all_to_all x1, blocking collectives, per_device(): lax.all_to_all(lesser, 'energy', split_axis=3, concat_axis=0, tiled=True)  33 us
    all_to_all x1, blocking collectives, per_device(): lax.all_to_all(greater, 'energy', split_axis=3, concat_axis=0, tiled=True)  28.8 us
    all_to_all x1, waiting for transfers between devices, per_device(): lax.all_to_all(sigma_more, 'energy', split_axis=0, concat_axis=3, tiled=T...  25.5 us
    all_gather x1, waiting for transfers between devices, per_device(): lax.all_gather(rows_more, 'momentum', axis=1, tiled=True)  20 us
    dot_general x16, matrix products, matrix_product(): return jnp.matmul(former, latter, preferred_element_type=jnp.float32)  9.88 us
    dot_general x1, matrix products, scattering(): jnp.einsum('jksq,sqxab->jkxab', mixer_less, less_part.astype(jnp.float32)...  9.66 us
    dot_general x1, matrix products, scattering(): jnp.einsum('jksq,sqxab->jkxab', mixer_more, more_part.astype(jnp.float32)...  9.66 us
    all_to_all x1, starting transfers between devices, per_device(): lax.all_to_all(sigma_more, 'energy', split_axis=0, concat_axis=3, tiled=T...  5.52 us
  transfers between devices with their start and end apart: 4, of which 3 were waited for; matrix products, arithmetic and copies ran while one was open for 15% of the time, Pallas kernels for 0%

commit v1 on v0

--- a/solution.py
+++ b/solution.py
@@ -2,6 +2,29 @@
 import jax.numpy as jnp
 from jax import lax
 from jax.sharding import PartitionSpec as P
+
+
+def in_blocks(x, dim, size):
+    before, after = (x.shape[:dim], x.shape[dim + 1 :])
+    return jnp.moveaxis(x.reshape(*before, size, -1, *after), dim, 0)
+
+
+def laid_out(blocks, dim):
+    blocks = jnp.moveaxis(blocks, 0, dim)
+    shape = blocks.shape
+    return blocks.reshape(*shape[:dim], shape[dim] * shape[dim + 1], *shape[dim + 2 :])
+
+
+def exchange_directly(x, axis, split_dim, concat_dim):
+    count, here = (lax.axis_size(axis), lax.axis_index(axis))
+    blocks = in_blocks(x, split_dim, count)
+    result = blocks
+    for step in range(1, count):
+        target, source = ((here + step) % count, (here - step) % count)
+        sent = lax.dynamic_index_in_dim(blocks, target, 0)
+        other = lax.ppermute(sent, axis, [(i, (i + step) % count) for i in range(count)])
+        result = lax.dynamic_update_slice_in_dim(result, other, source, axis=0)
+    return laid_out(result, concat_dim)
 
 
 def matrix_product(former, latter):
@@ -74,7 +97,7 @@
     sigma_more = (add_more * factor).astype(jnp.bfloat16)
     sigma_less, sigma_more = (
         lax.all_to_all(sigma_less, "energy", split_axis=0, concat_axis=3, tiled=True),
-        lax.all_to_all(sigma_more, "energy", split_axis=0, concat_axis=3, tiled=True),
+        exchange_directly(sigma_more, "energy", 0, 3),
     )
     sigma_ret = ((sigma_more.astype(jnp.float32) - sigma_less.astype(jnp.float32)) * 0.5).astype(
         jnp.bfloat16

time: 180 us -> 209 us (1.16)
  the two profiles are of different devices: /device:TPU:0 before, /device:TPU:20 now
where the time goes in v1:
time: 209 us; the launch traced here: 208 us
  blocking collectives  57.5 us (28%)
  starting transfers between devices  34.1 us (16%)
  local copies, waits for them, and re-layouts  34 us (16%)
  waiting for transfers between devices  33.9 us (16%)
  matrix products  29.6 us (14%)
  between operations  14.4 us (7%)
  other arithmetic  4.65 us (2%)
    all_to_all x1, blocking collectives, per_device(): lax.all_to_all(greater, 'energy', split_axis=3, concat_axis=0, tiled=True)  29.1 us
    all_to_all x1, blocking collectives, per_device(): lax.all_to_all(lesser, 'energy', split_axis=3, concat_axis=0, tiled=True)  28.4 us
    ppermute x7, starting transfers between devices, exchange_directly(): lax.ppermute(sent, axis, [(i, (i + step) % count) for i in range(count)])  28 us
    dynamic_update_slice x7, local copies, waits for them, and re-layouts, exchange_directly(): result = lax.dynamic_update_slice_in_dim(result, other, source, axis=0)  20.7 us
    all_gather x1, waiting for transfers between devices, per_device(): lax.all_gather(rows_more, 'momentum', axis=1, tiled=True)  19.5 us
    ppermute x7, waiting for transfers between devices, exchange_directly(): lax.ppermute(sent, axis, [(i, (i + step) % count) for i in range(count)])  10.8 us
    dot_general x16, matrix products, matrix_product(): return jnp.matmul(former, latter, preferred_element_type=jnp.float32)  9.88 us
    dot_general x1, matrix products, scattering(): jnp.einsum('jksq,sqxab->jkxab', mixer_less, less_part.astype(jnp.float32)...  9.66 us
  transfers between devices with their start and end apart: 10, of which 4 were waited for; matrix products, arithmetic and copies ran while one was open for 24% of the time, Pallas kernels for 0%

profile of v1, /device:TPU:20, one launch (start us, length us, event | category | flops | bytes accessed | tf_op | source)
XLA Modules:
  0.0 208.1 jit_solution(15639654489243674358)
XLA Ops:
  7.2 0.0 all-gather.5.cloned.1.call-start
  7.2 2.3 %copy.29 = bf16[1,1,2,512,512]{4,2,1,0,3:T(2,128)(2,1)S(1)} copy(bf16[1,1,2,512,512]{4,3,2,1,0:T(8,128)(2,1)} %param.6) | data formatting | bytes 2097152 | tf_op args[0]
  9.5 28.4 %all_to_all.51 = bf16[1,1,2,512,512]{4,2,1,0,3:T(2,128)(2,1)S(1)} all-to-all(bf16[1,1,2,512,512]{4,2,1,0,3:T(2,128)(2,1)S(1)} %copy.29), channel_id=1, replica_groups=mesh['energy'=8,'momentum'=4] {'energy'}, dimensions={3} | all-to-all | bytes 2097152 | tf_op jit(solution)/shard_map/all_to_all | solution.py:85
  38.0 1.5 copy.68
  39.5 0.0 all-gather.5.cloned.1.call-update
  39.5 0.0 all-gather.7.cloned.1.call-start
  39.6 1.1 copy.36
  40.7 29.1 %all_to_all.52 = bf16[1,1,2,512,512]{4,2,1,0,3:T(2,128)(2,1)S(1)} all-to-all(bf16[1,1,2,512,512]{4,2,1,0,3:T(2,128)(2,1)S(1)} %copy.36), channel_id=1, replica_groups=mesh['energy'=8,'momentum'=4] {'energy'}, dimensions={3} | all-to-all | bytes 2097152 | tf_op jit(solution)/shard_map/all_to_all | solution.py:86
  69.8 1.5 copy.67
  71.3 0.0 all-gather.7.cloned.1.call-update
  71.4 0.7 fusion.68
  72.1 0.1 fusion.65
  72.2 0.1 add_bitcast_fusion
  72.2 0.2 convolution_bitcast_fusion.1
  72.5 3.6 %all-gather.5.cloned.1.call-done = bf16[8,4,1,2,64,512]{5,0,1,4,3,2:T(8,128)(2,1)} async-done(((bf16[8,1,1,2,64,512]{5,0,1,4,3,2:T(8,128)(2,1)}), bf16[8,4,1,2,64,512]{5,0,1,4,3,2:T(8,128)(2,1)}) %all-gather.5.cloned.1.call-update) | async-done | bytes 4194320 | tf_op jit(solution)/shard_map/all_gather | solution.py:90
  76.0 9.7 %fusion.15 = bf16[8,1,2,64,512]{4,0,3,2,1:T(8,128)(2,1)S(1)} fusion(bf16[8,4,1,2,64,512]{5,0,1,4,3,2:T(8,128)(2,1)} %all-gather.5.cloned.1.call-done, f32[8,8,4,1,1]{1,2,0,4,3:T(4,128)S(1)} %convolution_bitcast_fusion.1), kind=kOutput, calls=%fused_computation.24 | convolution fusion | flops 202375168 | bytes 5243904 | tf_op jit(solution)/shard_map/jksq,sqxab->jkxab/dot_general | solution.py:63
  85.7 1.3 copy.33
  87.0 6.0 %all-to-all-start.1 = ((bf16[8,1,2,64,512]{4,3,2,1,0:T(8,128)(2,1)}), bf16[8,1,2,64,512]{4,3,2,1,0:T(8,128)(2,1)S(1)}, u32[]{:S(2)}, u32[]{:S(2)}) async-start(bf16[8,1,2,64,512]{4,3,2,1,0:T(8,128)(2,1)} %copy.33), calls=%async_computation.1 | async-start | bytes 2097152 | tf_op jit(solution)/shard_map/all_to_all | solution.py:99
  93.0 0.2 convolution_bitcast_fusion
  93.2 19.5 %all-gather.7.cloned.1.call-done = bf16[8,4,1,2,64,512]{5,0,1,4,3,2:T(8,128)(2,1)} async-done(((bf16[8,1,1,2,64,512]{5,0,1,4,3,2:T(8,128)(2,1)}), bf16[8,4,1,2,64,512]{5,0,1,4,3,2:T(8,128)(2,1)}) %all-gather.7.cloned.1.call-update) | async-done | bytes 4194320 | tf_op jit(solution)/shard_map/all_gather | solution.py:91
  112.7 9.7 %fusion.5 = bf16[8,2,64,512]{3,0,2,1:T(8,128)(2,1)S(1)} fusion(bf16[8,4,1,2,64,512]{5,0,1,4,3,2:T(8,128)(2,1)} %all-gather.7.cloned.1.call-done, f32[8,8,4,1,1]{1,2,0,4,3:T(4,128)S(1)} %convolution_bitcast_fusion), kind=kOutput, calls=%fused_computation.14 | convolution fusion | flops 202375168 | bytes 5243904 | tf_op jit(solution)/shard_map/jksq,sqxab->jkxab/dot_general | solution.py:69
  122.4 2.9 %dynamic-slice_bitcast_fusion = (bf16[1,1,1,2,64,512]{5,0,4,3,2,1:T(2,128)(2,1)}, bf16[1,1,1,2,64,512]{5,0,4,3,2,1:T(2,128)(2,1)}, bf16[1,1,1,2,64,512]{5,0,4,3,...) fusion(bf16[8,2,64,512]{3,0,2,1:T(8,128)(2,1)S(1)} %fusion.5, ...), kind=kLoop, calls=%fused_computation.79 | loop fusion | bytes 1835036 | tf_op jit(solution)/shard_map/jit(dynamic_index_in_dim)/dynamic_slice | solution.py:24
  125.2 1.5 collective-permute-start.1
  126.7 0.5 collective-permute-start
  127.2 1.5 collective-permute-start.4
  128.7 2.3 %collective-permute-start.2 = (bf16[1,1,1,2,64,512]{5,0,4,3,2,1:T(2,128)(2,1)}, bf16[1,1,1,2,64,512]{5,0,4,3,2,1:T(2,128)(2,1)}, u32[]{:S(2)}, u32[]{:S(2)}) collective-permute-start(bf16[1,1,1,2,64,512]{5,0,4,3,2,1:T(2,128)(2,1)} %get-tuple-element.10), channel_id=1, source_target_pairs={{0,12},{4,16},{8,20},{12,24},{16,28},{20,0},{24,4},{28,8},{1,13},{... | collective-permute-start | bytes 393224 | tf_op jit(solution)/shard_map/ppermute | solution.py:25
  131.0 1.5 collective-permute-start.3
  132.5 1.8 collective-permute-done.1
  134.4 0.5 collective-permute-start.5
  134.9 9.0 %collective-permute-done = bf16[1,1,1,2,64,512]{5,0,4,3,2,1:T(2,128)(2,1)} collective-permute-done((bf16[1,1,1,2,64,512]{5,0,4,3,2,1:T(2,128)(2,1)S(1)}, bf16[1,1,1,2,64,512]{5,0,4,3,2,1:T(2,128)(2,1)}, u32[]{:S(2)}, u32[]{:S(2)}) %collective-permute-start) | collective-permute-done | bytes 131104 | tf_op jit(solution)/shard_map/ppermute | solution.py:25
  143.9 20.1 %collective-permute-start.6 = (bf16[1,1,1,2,64,512]{5,0,4,3,2,1:T(2,128)(2,1)}, bf16[1,1,1,2,64,512]{5,0,4,3,2,1:T(2,128)(2,1)S(1)}, u32[]{:S(2)}, u32[]{:S(2)}) collective-permute-start(bf16[1,1,1,2,64,512]{5,0,4,3,2,1:T(2,128)(2,1)} %get-tuple-element.6), channel_id=1, source_target_pairs={{0,28},{4,0},{8,4},{12,8},{16,12},{20,16},{24,20},{28,24},{1,29},{... | collective-permute-start | bytes 393224 | tf_op jit(solution)/shard_map/ppermute | solution.py:25
  164.0 4.4 %dynamic_update_slice.21 = bf16[8,1,1,2,64,512]{5,0,4,3,2,1:T(8,128)(2,1)S(1)} dynamic-update-slice(bf16[8,1,1,2,64,512]{5,0,4,3,2,1:T(8,128)(2,1)S(1)} %bitcast.191, bf16[1,1,1,2,64,512]{5,0,4,3,2,1:T(2,128)(2,1)} %collective-permute-done, s32[]{:T(128)S(6)} %select_n.109, s32[]{:T(128)} %constant.102.clone.1, s32[]{:T(128)} %constant.102.clone.1, s32[]{:T(128)} %constant.102.clone.1, ...) | dynamic-update-slice | bytes 262148 | tf_op jit(solution)/shard_map/dynamic_update_slice | solution.py:26
  168.5 2.4 %dynamic_update_slice.22 = bf16[8,1,1,2,64,512]{5,0,4,3,2,1:T(8,128)(2,1)S(1)} dynamic-update-slice(bf16[8,1,1,2,64,512]{5,0,4,3,2,1:T(8,128)(2,1)S(1)} %dynamic_update_slice.21, bf16[1,1,1,2,64,512]{5,0,4,3,2,1:T(2,128)(2,1)S(1)} %collective-permute-done.1, s32[]{:T(128)S(6)} %select_n.113, s32[]{:T(128)} %constant.102.clone.1, s32[]{:T(128)} %constant.102.clone.1, s32[]{:T(128)} %constant.102.clone.1, ...) | dynamic-update-slice | bytes 262148 | tf_op jit(solution)/shard_map/dynamic_update_slice | solution.py:26
  170.9 4.5 %dynamic_update_slice.23 = bf16[8,1,1,2,64,512]{5,0,4,3,2,1:T(8,128)(2,1)S(1)} dynamic-update-slice(bf16[8,1,1,2,64,512]{5,0,4,3,2,1:T(8,128)(2,1)S(1)} %dynamic_update_slice.22, bf16[1,1,1,2,64,512]{5,0,4,3,2,1:T(2,128)(2,1)} %collective-permute-done.2, s32[]{:T(128)S(6)} %select_n.117, s32[]{:T(128)} %constant.102.clone.1, s32[]{:T(128)} %constant.102.clone.1, s32[]{:T(128)} %constant.102.clone.1, ...) | dynamic-update-slice | bytes 262148 | tf_op jit(solution)/shard_map/dynamic_update_slice | solution.py:26
  175.3 2.4 %dynamic_update_slice.24 = bf16[8,1,1,2,64,512]{5,0,4,3,2,1:T(8,128)(2,1)S(1)} dynamic-update-slice(bf16[8,1,1,2,64,512]{5,0,4,3,2,1:T(8,128)(2,1)S(1)} %dynamic_update_slice.23, bf16[1,1,1,2,64,512]{5,0,4,3,2,1:T(2,128)(2,1)S(1)} %collective-permute-done.3, s32[]{:T(128)S(6)} %select_n.121, s32[]{:T(128)} %constant.102.clone.1, s32[]{:T(128)} %constant.102.clone.1, s32[]{:T(128)} %constant.102.clone.1, ...) | dynamic-update-slice | bytes 262148 | tf_op jit(solution)/shard_map/dynamic_update_slice | solution.py:26
  177.7 2.4 %dynamic_update_slice.25 = bf16[8,1,1,2,64,512]{5,0,4,3,2,1:T(8,128)(2,1)S(1)} dynamic-update-slice(bf16[8,1,1,2,64,512]{5,0,4,3,2,1:T(8,128)(2,1)S(1)} %dynamic_update_slice.24, bf16[1,1,1,2,64,512]{5,0,4,3,2,1:T(2,128)(2,1)S(1)} %collective-permute-done.4, s32[]{:T(128)S(6)} %select_n.125, s32[]{:T(128)} %constant.102.clone.1, s32[]{:T(128)} %constant.102.clone.1, s32[]{:T(128)} %constant.102.clone.1, ...) | dynamic-update-slice | bytes 262148 | tf_op jit(solution)/shard_map/dynamic_update_slice | solution.py:26
  180.1 2.4 %dynamic_update_slice.26 = bf16[8,1,1,2,64,512]{5,0,4,3,2,1:T(8,128)(2,1)S(1)} dynamic-update-slice(bf16[8,1,1,2,64,512]{5,0,4,3,2,1:T(8,128)(2,1)S(1)} %dynamic_update_slice.25, bf16[1,1,1,2,64,512]{5,0,4,3,2,1:T(2,128)(2,1)S(1)} %collective-permute-done.5, s32[]{:T(128)S(6)} %select_n.129, s32[]{:T(128)} %constant.102.clone.1, s32[]{:T(128)} %constant.102.clone.1, s32[]{:T(128)} %constant.102.clone.1, ...) | dynamic-update-slice | bytes 262148 | tf_op jit(solution)/shard_map/dynamic_update_slice | solution.py:26
  182.5 2.4 %dynamic_update_slice.27 = bf16[8,1,1,2,64,512]{5,0,4,3,2,1:T(8,128)(2,1)S(1)} dynamic-update-slice(bf16[8,1,1,2,64,512]{5,0,4,3,2,1:T(8,128)(2,1)S(1)} %dynamic_update_slice.26, bf16[1,1,1,2,64,512]{5,0,4,3,2,1:T(2,128)(2,1)S(1)} %collective-permute-done.6, s32[]{:T(128)S(6)} %select_n.133, s32[]{:T(128)} %constant.102.clone.1, s32[]{:T(128)} %constant.102.clone.1, s32[]{:T(128)} %constant.102.clone.1, ...) | dynamic-update-slice | bytes 262148 | tf_op jit(solution)/shard_map/dynamic_update_slice | solution.py:26
  184.9 0.3 copy.40
  185.2 0.5 copy.44
  185.7 0.1 copy.34
  185.8 0.8 copy.43
  186.6 0.3 multiply_convert_fusion
  187.0 0.3 pad_maximum_fusion
  187.3 0.9 copy-done
  188.2 1.0 fusion.14
  189.2 1.0 fusion.13
  190.2 1.1 fusion.12
  191.3 1.1 fusion.11
  192.3 0.3 fusion.32
  192.6 0.5 fusion.33
  193.1 0.5 fusion.37
  193.5 0.5 fusion.47
  194.0 0.5 fusion.49
  194.5 0.5 fusion.43
  195.0 0.5 fusion.45
  195.5 0.5 fusion.18
  196.0 0.5 fusion.19
  196.4 0.5 fusion.26
  196.9 0.5 fusion.27
  197.4 0.5 fusion.24
  197.9 0.5 fusion.25
  198.4 1.4 fusion.4
  199.8 1.5 pad_maximum_fusion.2
  (15 shorter events, 0.0 us)
Async XLA Ops:
  7.2 68.9 %all-gather.5.cloned.1.call-start = ((), (), s32[]{:S(2)}) async-start(), calls=%async_computation.3 | async-start | bytes 5242880 | tf_op jit(solution)/shard_map/all_gather | solution.py:90
  9.5 30.1 %copy-start.1 = (bf16[1,1,2,512,512]{4,3,2,1,0:T(8,128)(2,1)S(1)}, bf16[1,1,2,512,512]{4,3,2,1,0:T(8,128)(2,1)}, u32[]{:S(2)}) copy-start(bf16[1,1,2,512,512]{4,3,2,1,0:T(8,128)(2,1)} %param.7) | copy-start | bytes 3145732
  39.5 73.2 %all-gather.7.cloned.1.call-start = ((), (), s32[]{:S(2)}) async-start(), calls=%async_computation.4 | async-start | bytes 5242880 | tf_op jit(solution)/shard_map/all_gather | solution.py:91
  40.7 30.7 %copy-start.2 = (s32[2,2,8]{2,1,0:T(2,128)S(1)}, s32[2,2,8]{2,1,0:T(2,128)}, u32[]{:S(2)}) copy-start(s32[2,2,8]{2,1,0:T(2,128)} %param.10) | copy-start | bytes 388
  40.7 31.4 %copy-start.3 = (f32[2]{0:T(128)S(1)}, f32[2]{0:T(128)}, u32[]{:S(2)}) copy-start(f32[2]{0:T(128)} %param.9) | copy-start | bytes 28
  87.0 98.7 %all-to-all-start.1 = ((bf16[8,1,2,64,512]{4,3,2,1,0:T(8,128)(2,1)}), bf16[8,1,2,64,512]{4,3,2,1,0:T(8,128)(2,1)S(1)}, u32[]{:S(2)}, u32[]{:S(2)}) async-start(bf16[8,1,2,64,512]{4,3,2,1,0:T(8,128)(2,1)} %copy.33), calls=%async_computation.1 | async-start | bytes 2097152 | tf_op jit(solution)/shard_map/all_to_all | solution.py:99
  125.2 9.1 %collective-permute-start.1 = (bf16[1,1,1,2,64,512]{5,0,4,3,2,1:T(2,128)(2,1)S(1)}, bf16[1,1,1,2,64,512]{5,0,4,3,2,1:T(2,128)(2,1)S(1)}, u32[]{:S(2)}, u32[]{:S(2)}) collective-permute-start(bf16[1,1,1,2,64,512]{5,0,4,3,2,1:T(2,128)(2,1)S(1)} %get-tuple-element.11), channel_id=1, source_target_pairs={{0,8},{4,12},{8,16},{12,20},{16,24},{20,28},{24,0},{28,4},{1,9},{5... | collective-permute-start | bytes 393224 | tf_op jit(solution)/shard_map/ppermute | solution.py:25
  126.7 17.2 %collective-permute-start = (bf16[1,1,1,2,64,512]{5,0,4,3,2,1:T(2,128)(2,1)S(1)}, bf16[1,1,1,2,64,512]{5,0,4,3,2,1:T(2,128)(2,1)}, u32[]{:S(2)}, u32[]{:S(2)}) collective-permute-start(bf16[1,1,1,2,64,512]{5,0,4,3,2,1:T(2,128)(2,1)S(1)} %get-tuple-element.12), channel_id=1, source_target_pairs={{0,4},{4,8},{8,12},{12,16},{16,20},{20,24},{24,28},{28,0},{1,5},{5... | collective-permute-start | bytes 393224 | tf_op jit(solution)/shard_map/ppermute | solution.py:25
  127.2 50.5 %collective-permute-start.4 = (bf16[1,1,1,2,64,512]{5,0,4,3,2,1:T(2,128)(2,1)}, bf16[1,1,1,2,64,512]{5,0,4,3,2,1:T(2,128)(2,1)S(1)}, u32[]{:S(2)}, u32[]{:S(2)}) collective-permute-start(bf16[1,1,1,2,64,512]{5,0,4,3,2,1:T(2,128)(2,1)} %get-tuple-element.8), channel_id=1, source_target_pairs={{0,20},{4,24},{8,28},{12,0},{16,4},{20,8},{24,12},{28,16},{1,21},{... | collective-permute-start | bytes 393224 | tf_op jit(solution)/shard_map/ppermute | solution.py:25
  128.7 42.1 %collective-permute-start.2 = (bf16[1,1,1,2,64,512]{5,0,4,3,2,1:T(2,128)(2,1)}, bf16[1,1,1,2,64,512]{5,0,4,3,2,1:T(2,128)(2,1)}, u32[]{:S(2)}, u32[]{:S(2)}) collective-permute-start(bf16[1,1,1,2,64,512]{5,0,4,3,2,1:T(2,128)(2,1)} %get-tuple-element.10), channel_id=1, source_target_pairs={{0,12},{4,16},{8,20},{12,24},{16,28},{20,0},{24,4},{28,8},{1,13},{... | collective-permute-start | bytes 393224 | tf_op jit(solution)/shard_map/ppermute | solution.py:25
  131.0 44.3 %collective-permute-start.3 = (bf16[1,1,1,2,64,512]{5,0,4,3,2,1:T(2,128)(2,1)}, bf16[1,1,1,2,64,512]{5,0,4,3,2,1:T(2,128)(2,1)S(1)}, u32[]{:S(2)}, u32[]{:S(2)}) collective-permute-start(bf16[1,1,1,2,64,512]{5,0,4,3,2,1:T(2,128)(2,1)} %get-tuple-element.9), channel_id=1, source_target_pairs={{0,16},{4,20},{8,24},{12,28},{16,0},{20,4},{24,8},{28,12},{1,17},{... | collective-permute-start | bytes 393224 | tf_op jit(solution)/shard_map/ppermute | solution.py:25
  134.4 45.7 %collective-permute-start.5 = (bf16[1,1,1,2,64,512]{5,0,4,3,2,1:T(2,128)(2,1)}, bf16[1,1,1,2,64,512]{5,0,4,3,2,1:T(2,128)(2,1)S(1)}, u32[]{:S(2)}, u32[]{:S(2)}) collective-permute-start(bf16[1,1,1,2,64,512]{5,0,4,3,2,1:T(2,128)(2,1)} %get-tuple-element.7), channel_id=1, source_target_pairs={{0,24},{4,28},{8,0},{12,4},{16,8},{20,12},{24,16},{28,20},{1,25},{... | collective-permute-start | bytes 393224 | tf_op jit(solution)/shard_map/ppermute | solution.py:25
  143.9 38.6 %collective-permute-start.6 = (bf16[1,1,1,2,64,512]{5,0,4,3,2,1:T(2,128)(2,1)}, bf16[1,1,1,2,64,512]{5,0,4,3,2,1:T(2,128)(2,1)S(1)}, u32[]{:S(2)}, u32[]{:S(2)}) collective-permute-start(bf16[1,1,1,2,64,512]{5,0,4,3,2,1:T(2,128)(2,1)} %get-tuple-element.6), channel_id=1, source_target_pairs={{0,28},{4,0},{8,4},{12,8},{16,12},{20,16},{24,20},{28,24},{1,29},{... | collective-permute-start | bytes 393224 | tf_op jit(solution)/shard_map/ppermute | solution.py:25
  186.9 1.2 copy-start
Sparse Core Ops, SparseCore 0:
  39.7 36.3 all-gather.4
  78.2 34.4 all-gather.6
